TPU v7x, 32 devices: a whole 2x2x4 slice. The times are simulated.
32 devices in a mesh: member: 4 (over y, core), space: 8 (over z, x).
Axes of the slice: x: 2, y: 2, z: 4, core: 2. Of those that a mesh axis runs over, the one named last changes fastest.
Arguments:
- ensemble: float32 [256, 32, 2048], P('member', None, 'space'), may hold values from -6 to 6
- obs_weight: float32 [32, 8192], P(None, 'space'), may hold values from -1 to 1
- obs_value: float32 [8192], P('space'), may hold values from -6 to 6
- obs_rinv: float32 [8192], P('space'), may hold values from 0.5 to 4
- obs_column: int32 [8192], P('space'), may hold values from 0 to 255
- set_rows: int32 [32, 512], P('space'), may hold values from 0 to 1023
- set_count: int32 [32], P('space'), may hold values from 128 to 512, as said below
- neighbour: int32 [4, 2048], P(None, 'space'), may hold values from 0 to 3
- interp_weight: float32 [4, 2048], P(None, 'space'), may hold values from 0.1 to 1
Outputs:
- analysed: float32 [256, 32, 2048], P('member', None, 'space')
Inputs may be any that keep to these rules, and one draw needn't show every extreme that they name: `set_rows`: a row among the 1024 observations of the space index that owns the coarse point; coarse point j is owned by space index j // (member count). `set_count`: rows of a local set at or past its count are padding; some coarse point has the full 512 rows in every draw. `obs_column`: a column among the 256 columns of the space index that holds the observation. `neighbour`: a coarse point among those owned by the column's own space index, numbered from 0.
All inputs are finite; a program needn't handle non-finite values.
Results may differ from a plain program's by a relative error of at most 0.0035.
Values may be sent and summed in bfloat16 or wider, within the bound.
A program may use at most 64 MiB of HBM per device.

v0:
```python
import jax
import jax.numpy as jnp
from jax import lax
from jax.sharding import PartitionSpec as P

NS_ITERS = 5


highest = lax.Precision.HIGHEST


def make_transform(selected, obs_pick, rinv_pick, count):
    ens_size = selected.shape[0]
    set_len = selected.shape[1]
    obs_mean = jnp.mean(selected, axis=0)
    anomaly = selected - obs_mean[None, :]
    innovation = obs_pick - obs_mean
    in_set = jnp.arange(set_len, dtype=jnp.int32) < count
    set_weight = jnp.where(in_set, rinv_pick, jnp.zeros_like(rinv_pick))
    identity = jnp.eye(ens_size, dtype=selected.dtype)
    posterior = (ens_size - 1.0) * identity + jnp.dot(
        anomaly * set_weight[None, :], anomaly.T, precision=highest
    )
    frob_norm = jnp.sqrt(jnp.sum(posterior * posterior))
    iterate = posterior / frob_norm
    inverse = identity
    for turn_index in range(NS_ITERS):
        ns_step = 1.5 * identity - 0.5 * jnp.dot(inverse, iterate, precision=highest)
        iterate = jnp.dot(iterate, ns_step, precision=highest)
        inverse = jnp.dot(ns_step, inverse, precision=highest)
    drive_vec = jnp.dot(anomaly, set_weight * innovation, precision=highest)
    mean_weight = (
        jnp.dot(inverse, jnp.dot(inverse, drive_vec, precision=highest), precision=highest)
        / frob_norm
    )
    spread = inverse * jnp.sqrt((ens_size - 1.0) / frob_norm)
    return (spread + mean_weight[:, None]).astype(jnp.bfloat16)


def local(
    ensemble,
    obs_weight,
    obs_value,
    obs_rinv,
    obs_column,
    set_rows,
    set_count,
    neighbour,
    interp_weight,
):
    member_count = lax.axis_size("member")
    my_index = lax.axis_index("member")
    picked_vals = jnp.take(ensemble, obs_column, axis=2)
    observed = jnp.sum(picked_vals * obs_weight[None], axis=1)
    my_rows = lax.dynamic_index_in_dim(set_rows, my_index, 0, keepdims=False)
    my_count = lax.dynamic_index_in_dim(set_count, my_index, 0, keepdims=False)
    outgoing = jnp.take(observed, set_rows, axis=1)
    selected = lax.all_to_all(outgoing, "member", split_axis=1, concat_axis=0, tiled=True)[:, 0, :]
    transform = make_transform(
        selected, jnp.take(obs_value, my_rows), jnp.take(obs_rinv, my_rows), my_count
    )
    regrouped = lax.all_to_all(ensemble, "member", split_axis=1, concat_axis=0, tiled=True)
    ens_mean = jnp.mean(regrouped, axis=0)
    anomalies = (regrouped - ens_mean[None]).astype(jnp.bfloat16)
    norm_weight = interp_weight / jnp.sum(interp_weight, axis=0)[None, :]
    matches = neighbour[:, None, :] == jnp.arange(member_count, dtype=jnp.int32)[None, :, None]
    pointwise = jnp.sum(
        jnp.where(matches, norm_weight[:, None, :], jnp.zeros_like(norm_weight[:, None, :])), axis=0
    )

    def contribution(matrix, scale_row):
        product = jnp.einsum("kl,kvc->lvc", matrix, anomalies, preferred_element_type=jnp.float32)
        return product * scale_row[None, None, :]

    zero_sum = jnp.zeros(anomalies.shape, jnp.float32)
    everything = lax.all_gather(transform[None], "member", axis=0, tiled=True)

    def accumulate(which, running):
        return running + contribution(everything[which], pointwise[which])

    running_sum = lax.fori_loop(0, member_count, accumulate, zero_sum)
    analysed = ens_mean[None] + running_sum
    return lax.all_to_all(analysed, "member", split_axis=0, concat_axis=1, tiled=True)


def solution(mesh):
    placed = (
        P("member", None, "space"),
        P(None, "space"),
        P("space"),
        P("space"),
        P("space"),
        P("space", None),
        P("space"),
        P(None, "space"),
        P(None, "space"),
    )
    return jax.shard_map(
        local, mesh=mesh, in_specs=placed, out_specs=P("member", None, "space"), check_vma=False
    )
```

profile of v0, /device:TPU:1, one launch (start us, length us, event | category | flops | bytes accessed | tf_op | source)
XLA Modules:
  0.0 129.7 jit_solution(1444631955270202974)
XLA Ops:
  0.0 0.7 fusion.13
  0.7 0.7 compare_and_fusion.1
  1.4 0.7 fusion.12
  2.1 0.7 compare_and_fusion
  2.8 5.6 %copy.29 = f32[64,32,256]{0,1,2:T(8,128)} copy(f32[64,32,256]{2,1,0:T(8,128)} %param.13) | data formatting | bytes 4194304 | tf_op args[0]
  8.6 14.6 %gather_fusion = f32[1024,64,32]{1,2,0:T(8,128)} fusion(f32[64,32,256]{0,1,2:T(8,128)} %copy.29, s32[1024]{0:T(1024)S(1)} %fusion.13), kind=kCustom, calls=%fused_computation.2 | custom fusion | bytes 16781312 | tf_op jit(solution)/shard_map/jit(_take)/gather | solution.py:53
  23.2 8.3 %fusion.3 = f32[64,1024]{0,1:T(8,128)S(1)} fusion(f32[1024,64,32]{1,2,0:T(8,128)} %gather_fusion, f32[32,1024]{0,1:T(8,128)S(1)} %copy.30, pred[1024]{0:T(1024)(128)(4,1)S(1)} %compare_and_fusion.1), kind=kLoop, calls=%fused_computation.10 | loop fusion | flops 6225920 | bytes 8782848 | tf_op jit(solution)/shard_map/reduce_sum | solution.py:54
  31.5 5.5 %gather_fusion.1 = f32[2048,64]{1,0:T(8,128)S(1)} fusion(f32[64,1024]{0,1:T(8,128)S(1)} %fusion.3, s32[2048]{0:T(1024)S(1)} %broadcast_clamp_fusion), kind=kCustom, calls=%fused_computation.3 | custom fusion | bytes 1056768 | tf_op jit(solution)/shard_map/jit(_take)/gather | solution.py:57
  37.0 1.1 copy.31
  38.1 1.9 %select_bitcast_fusion = f32[64,4,512]{2,0,1:T(8,128)} fusion(f32[4,512,64]{1,2,0:T(8,128)} %copy.31, pred[4,512]{1,0:T(4,128)(4,1)S(1)} %compare_and_fusion), kind=kLoop, calls=%fused_computation.30 | loop fusion | flops 131072 | bytes 1050624 | tf_op jit(solution)/shard_map/jit(_take)/select_n | solution.py:57
  40.0 4.3 %all-to-all-start.1 = ((f32[64,4,512]{2,0,1:T(8,128)}), f32[64,4,512]{2,0,1:T(8,128)S(1)}, u32[]{:S(2)}, u32[]{:S(2)}) async-start(f32[64,4,512]{2,0,1:T(8,128)} %select_bitcast_fusion), calls=%async_computation.1 | async-start | bytes 1048576 | tf_op jit(solution)/shard_map/all_to_all | solution.py:58
  44.3 0.7 constant_dynamic-slice_fusion.1
  45.0 2.5 %copy.28 = f32[64,32,256]{2,0,1:T(8,128)} copy(f32[64,32,256]{2,1,0:T(8,128)S(1)} %copy-done.2) | data formatting | bytes 4194304 | tf_op args[0]
  47.6 2.3 %gather_fusion.2 = f32[512]{0:T(512)S(1)} fusion(f32[1024]{0:T(1024)S(1)} %copy-done, s32[1024]{0:T(1024)S(1)} %pad_clamp_fusion), kind=kCustom, calls=%fused_computation.clone | custom fusion | bytes 6144 | tf_op jit(solution)/shard_map/jit(_take)/gather | solution.py:60
  49.9 2.3 %gather_fusion.3 = f32[512]{0:T(512)S(1)} fusion(f32[1024]{0:T(1024)S(1)} %copy-done.1, s32[1024]{0:T(1024)S(1)} %pad_clamp_fusion), kind=kCustom, calls=%fused_computation.1.clone | custom fusion | bytes 6144 | tf_op jit(solution)/shard_map/jit(_take)/gather | solution.py:60
  52.2 0.6 dynamic_slice.22
  52.9 4.7 %all-to-all-start = ((f32[64,32,256]{2,0,1:T(8,128)}), f32[64,32,256]{2,0,1:T(8,128)}, u32[]{:S(2)}, u32[]{:S(2)}) async-start(f32[64,32,256]{2,0,1:T(8,128)} %copy.28), calls=%async_computation | async-start | bytes 4194304 | tf_op jit(solution)/shard_map/all_to_all | solution.py:62
  57.6 0.6 fusion.14
  58.4 1.2 multiply_reduce_fusion
  60.3 0.3 fusion.9
  60.6 0.4 fusion.11
  61.0 0.3 fusion.10
  61.3 0.4 fusion.8
  61.7 0.4 fusion.16
  62.0 0.4 fusion.15
  62.4 0.4 fusion.7
  62.8 0.4 fusion.18
  63.2 0.4 fusion.17
  63.6 0.4 fusion.6
  64.0 0.4 fusion.20
  64.4 0.4 fusion.19
  64.8 0.4 fusion.5
  65.3 0.5 convolution_bitcast_fusion.1
  65.8 0.4 fusion.21
  66.2 0.3 convolution_bitcast_fusion
  66.5 0.3 fusion.22
  67.0 20.2 %all-gather = bf16[1024,256]{1,0:T(8,128)(2,1)} all-gather(bf16[256,256]{1,0:T(8,128)(2,1)S(1)} %add_convert_fusion), channel_id=2, replica_groups=mesh['member'=4,'space'=8] {'member'}, dimensions={0}, use_global_device_ids=true | all-gather | bytes 655360 | tf_op jit(solution)/shard_map/all_gather | solution.py:76
  87.2 1.7 %reduce_sum.54 = f32[8,256]{1,0:T(8,128)S(1)} reduce(f32[4,64,8,256]{3,1,2,0:T(8,128)} %bitcast.1, f32[]{:T(128)} %constant.83.clone.1), dimensions={0,1}, to_apply=%region_0.1 | reduce | flops 522240 | bytes 2105348 | tf_op jit(solution)/shard_map/reduce_sum | solution.py:63
  89.0 2.8 %copy.32 = f32[4,64,8,256]{3,2,1,0:T(8,128)S(1)} copy(f32[4,64,8,256]{3,1,2,0:T(8,128)} %bitcast.1) | data formatting | bytes 4194304 | tf_op jit(solution)/shard_map/all_to_all | solution.py:62
  92.0 0.2 copy.34
  92.2 7.3 %while.14 = (s32[]{:T(128)}, f32[256,8,256]{2,0,1:T(8,128)S(1)}, bf16[4,256,256]{2,1,0:T(8,128)(2,1)}, bf16[256,8,256]{2,0,1:T(8,128)(2,1)S(1)}, f32[4,256]{1,0:T(4,128)S(1)}, /*index=5*/s32[]{:T(128)}, s32[]{:T(128)}) while((s32[]{:T(128)}, f32[256,8,256]{2,0,1:T(8,128)S(1)}, bf16[4,256,256]{2,1,0:T(8,128)(2,1)}, ...), condition=%wide.region_7.9_spmd.clone, body=%wide.region_6.8_spmd.clone.sunk | while | flops 270008320 | bytes 5377627 | solution.py:81
  92.2 1.8 %select_add_fusion.2 = f32[256,8,256]{2,0,1:T(8,128)S(1)} fusion(f32[256,8,256]{2,0,1:T(8,128)S(1)} %get-tuple-element.195, bf16[256,8,256]{2,0,1:T(8,128)(2,1)S(1)} %get-tuple-element.204, f32[256]{0:T(256)S(1)} %bitcast.94, pred[]{:T(512)S(6)} %compare.3, bf16[4,256,256]{2,1,0:T(8,128)(2,1)} %get-tuple-element.203, s32[]{:T(128)} %get-tuple-element.194), kind=kOutput, calls=%fused_computation.4.clone.1 | convolution fusion | flops 270008320 | bytes 5375489 | tf_op jit(solution)/shard_map/while/body/eval_jaxpr/kl,kvc->lvc/dot_general | solution.py:72
  94.1 1.8 %select_add_fusion.2 = f32[256,8,256]{2,0,1:T(8,128)S(1)} fusion(f32[256,8,256]{2,0,1:T(8,128)S(1)} %get-tuple-element.195, bf16[256,8,256]{2,0,1:T(8,128)(2,1)S(1)} %get-tuple-element.204, f32[256]{0:T(256)S(1)} %bitcast.94, pred[]{:T(512)S(6)} %compare.3, bf16[4,256,256]{2,1,0:T(8,128)(2,1)} %get-tuple-element.203, s32[]{:T(128)} %get-tuple-element.194), kind=kOutput, calls=%fused_computation.4.clone.1 | convolution fusion | flops 270008320 | bytes 5375489 | tf_op jit(solution)/shard_map/while/body/eval_jaxpr/kl,kvc->lvc/dot_general | solution.py:72
  95.9 1.8 %select_add_fusion.2 = f32[256,8,256]{2,0,1:T(8,128)S(1)} fusion(f32[256,8,256]{2,0,1:T(8,128)S(1)} %get-tuple-element.195, bf16[256,8,256]{2,0,1:T(8,128)(2,1)S(1)} %get-tuple-element.204, f32[256]{0:T(256)S(1)} %bitcast.94, pred[]{:T(512)S(6)} %compare.3, bf16[4,256,256]{2,1,0:T(8,128)(2,1)} %get-tuple-element.203, s32[]{:T(128)} %get-tuple-element.194), kind=kOutput, calls=%fused_computation.4.clone.1 | convolution fusion | flops 270008320 | bytes 5375489 | tf_op jit(solution)/shard_map/while/body/eval_jaxpr/kl,kvc->lvc/dot_general | solution.py:72
  97.7 1.8 %select_add_fusion.2 = f32[256,8,256]{2,0,1:T(8,128)S(1)} fusion(f32[256,8,256]{2,0,1:T(8,128)S(1)} %get-tuple-element.195, bf16[256,8,256]{2,0,1:T(8,128)(2,1)S(1)} %get-tuple-element.204, f32[256]{0:T(256)S(1)} %bitcast.94, pred[]{:T(512)S(6)} %compare.3, bf16[4,256,256]{2,1,0:T(8,128)(2,1)} %get-tuple-element.203, s32[]{:T(128)} %get-tuple-element.194), kind=kOutput, calls=%fused_computation.4.clone.1 | convolution fusion | flops 270008320 | bytes 5375489 | tf_op jit(solution)/shard_map/while/body/eval_jaxpr/kl,kvc->lvc/dot_general | solution.py:72
  99.5 1.2 copy_add_fusion
  100.7 27.3 %all_to_all.51 = f32[256,8,256]{2,1,0:T(8,128)S(1)} all-to-all(f32[256,8,256]{2,1,0:T(8,128)S(1)} %copy_add_fusion), channel_id=1, replica_groups=mesh['member'=4,'space'=8] {'member'}, dimensions={0} | all-to-all | bytes 4194304 | tf_op jit(solution)/shard_map/all_to_all | solution.py:83
  128.0 1.6 %copy.41 = f32[64,4,8,256]{3,2,1,0:T(8,128)} copy(f32[64,4,8,256]{3,2,0,1:T(8,128)S(1)} %bitcast.89) | data formatting | bytes 4194304 | tf_op jit(solution)/shard_map/all_to_all | solution.py:83
  (36 shorter events, 0.9 us)
Async XLA Ops:
  0.0 47.6 %copy-start = (f32[1024]{0:T(1024)S(1)}, f32[1024]{0:T(1024)}, u32[]{:S(2)}) copy-start(f32[1024]{0:T(1024)} %param.16) | copy-start | bytes 12292
  2.8 5.6 %copy-start.3 = (f32[32,1024]{1,0:T(8,128)S(1)}, f32[32,1024]{1,0:T(8,128)}, u32[]{:S(2)}) copy-start(f32[32,1024]{1,0:T(8,128)} %param.14) | copy-start | bytes 393220
  37.0 8.0 %copy-start.2 = (f32[64,32,256]{2,1,0:T(8,128)S(1)}, f32[64,32,256]{2,1,0:T(8,128)}, u32[]{:S(2)}) copy-start(f32[64,32,256]{2,1,0:T(8,128)} %param.13) | copy-start | bytes 6291460
  40.0 12.9 %all-to-all-start.1 = ((f32[64,4,512]{2,0,1:T(8,128)}), f32[64,4,512]{2,0,1:T(8,128)S(1)}, u32[]{:S(2)}, u32[]{:S(2)}) async-start(f32[64,4,512]{2,0,1:T(8,128)} %select_bitcast_fusion), calls=%async_computation.1 | async-start | bytes 1048576 | tf_op jit(solution)/shard_map/all_to_all | solution.py:58
  47.6 2.3 %copy-start.1 = (f32[1024]{0:T(1024)S(1)}, f32[1024]{0:T(1024)}, u32[]{:S(2)}) copy-start(f32[1024]{0:T(1024)} %param.15) | copy-start | bytes 12292
  47.6 4.6 %copy-start.6 = (s32[4]{0:T(128)S(1)}, s32[4]{0:T(128)}, u32[]{:S(2)}) copy-start(s32[4]{0:T(128)} %param.19) | copy-start | bytes 52
  47.6 5.2 %copy-start.4 = (f32[4,256]{1,0:T(4,128)S(1)}, f32[4,256]{1,0:T(4,128)}, u32[]{:S(2)}) copy-start(f32[4,256]{1,0:T(4,128)} %param.21) | copy-start | bytes 12292
  47.6 5.3 %copy-start.5 = (s32[4,256]{1,0:T(4,128)S(1)}, s32[4,256]{1,0:T(4,128)}, u32[]{:S(2)}) copy-start(s32[4,256]{1,0:T(4,128)} %param.20) | copy-start | bytes 12292
  52.9 34.3 %all-to-all-start = ((f32[64,32,256]{2,0,1:T(8,128)}), f32[64,32,256]{2,0,1:T(8,128)}, u32[]{:S(2)}, u32[]{:S(2)}) async-start(f32[64,32,256]{2,0,1:T(8,128)} %copy.28), calls=%async_computation | async-start | bytes 4194304 | tf_op jit(solution)/shard_map/all_to_all | solution.py:62
where the time goes:
time: 131 us; the launch traced here: 130 us
  blocking collectives  47.5 us (36%)
  local copies, waits for them, and re-layouts  40.1 us (31%)
  other arithmetic  17.2 us (13%)
  matrix products  14.6 us (11%)
  starting transfers between devices  8.97 us (7%)
    all_to_all x1, blocking collectives, local(): lax.all_to_all(analysed, 'member', split_axis=0, concat_axis=1, tiled=True)  27.3 us
    all_gather x1, blocking collectives, local(): everything = lax.all_gather(transform[None], 'member', axis=0, tiled=True)  20.2 us
    gather x1, local copies, waits for them, and re-layouts, local(): picked_vals = jnp.take(ensemble, obs_column, axis=2)  14.6 us
    unnamed x19, local copies, waits for them, and re-layouts  8.56 us
    reduce_sum x1, other arithmetic, local(): observed = jnp.sum(picked_vals * obs_weight[None], axis=1)  8.27 us
    dot_general x4, matrix products, contribution(): jnp.einsum('kl,kvc->lvc', matrix, anomalies, preferred_element_type=jnp.f...  7.16 us
    gather x2, local copies, waits for them, and re-layouts, local(): outgoing = jnp.take(observed, set_rows, axis=1)  6.58 us
    all_to_all x1, starting transfers between devices, local(): lax.all_to_all(ensemble, 'member', split_axis=1, concat_axis=0, tiled=True)  4.68 us
  transfers between devices with their start and end apart: 2, of which 0 were waited for; matrix products, arithmetic and copies ran while one was open for 13% of the time, Pallas kernels for 0%

commit v1 on v0

v1 whole, which is shorter than its diff:
```python
import functools

import jax
import jax.numpy as jnp
from jax import lax
from jax.experimental import pallas as pl
from jax.experimental.pallas import tpu as pltpu
from jax.sharding import PartitionSpec as P

NS_ITERS = 5
CHUNKS = 8
MESH = pl.DeviceIdType.MESH
f32 = jnp.float32
bf16 = jnp.bfloat16


def split(x):
    high = x.astype(bf16)
    return high, (x - high.astype(f32)).astype(bf16)


def mm(x, y):
    return jnp.dot(x, y, preferred_element_type=f32)


def mm_t(x, y):
    return lax.dot_general(x, y, (((1,), (1,)), ((), ())), preferred_element_type=f32)


def mm3(x, y):
    return mm(x[0], y[0]) + (mm(x[0], y[1]) + mm(x[1], y[0]))


def kernel(
    n,
    block,
    ens_ref,
    weight_ref,
    value_ref,
    rinv_ref,
    column_ref,
    rows_ref,
    count_ref,
    near_ref,
    interp_ref,
    out_ref,
    held,
    result_held,
    sums,
    mean,
    anom,
    seen,
    acc,
    hot,
    turn,
    turns,
    sum_send,
    sum_recv,
    turn_send,
    turn_recv,
    own_send,
    own_recv,
    far_send,
    far_recv,
    pass_send,
    pass_recv,
    held_sem,
    result_sem,
):
    me = lax.axis_index("member")
    chips = n // 2
    chip, core = me // 2, lax.rem(me, 2)
    partner = chip * 2 + (1 - core)
    nv = mean.shape[0]
    members = n * block
    group = nv // CHUNKS
    n_obs = weight_ref.shape[1]
    n_set = rows_ref.shape[1]

    def peer(step):
        return lax.rem(me + step, n)

    def far(step):
        return lax.rem(chip + step, chips) * 2 + core

    def came(step):
        return lax.rem(chip + chips - step, chips) * 2 + core

    def span(index):
        return pl.ds(pl.multiple_of(index * block, block), block)

    def remote(src, dst, send, recv, to):
        return pltpu.make_async_remote_copy(
            src_ref=src,
            dst_ref=dst,
            send_sem=send,
            recv_sem=recv,
            device_id={"member": to},
            device_id_type=MESH,
        )

    lanes = held.shape[0]
    loads = [
        pltpu.make_async_copy(
            ens_ref.at[:, :, pl.ds(lane * 128, 128)], held.at[lane], held_sem.at[lane]
        )
        for lane in range(lanes)
    ]
    for copy in loads:
        copy.start()

    barrier = pltpu.get_barrier_semaphore()
    for step in range(1, n):
        pl.semaphore_signal(barrier, inc=1, device_id={"member": peer(step)}, device_id_type=MESH)
    pl.semaphore_wait(barrier, n - 1)

    def view(part, index):
        if part == 0:
            return seen.at[span(index), :]
        return anom.at[pl.ds((part - 1) * group, group), span(index), :]

    def own_copy(part):
        ref = view(part, me)
        return remote(ref, ref, own_send.at[part], own_recv.at[part], partner)

    def far_copy(part, step):
        ref = view(part, me)
        return remote(ref, ref, far_send.at[part, step - 1], far_recv.at[part, step - 1], far(step))

    def pass_copy(part, step):
        ref = view(part, came(step))
        return remote(ref, ref, pass_send.at[part, step - 1], pass_recv.at[part, step - 1], partner)

    def send(part):
        for step in range(1, chips):
            far_copy(part, step).start()
        own_copy(part).start()

    def forward(part):
        for step in range(1, chips):
            far_copy(part, step).wait_recv()
            pass_copy(part, step).start()

    def arrive(part):
        own_copy(part).wait_recv()
        for step in range(1, chips):
            pass_copy(part, step).wait_recv()

    for lane in range(lanes):
        loads[lane].wait()
        total = held[lane, 0]
        for k in range(1, block):
            total = total + held[lane, k]
        sums[me, :, pl.ds(lane * 128, 128)] = total
    sum_copies = [
        remote(sums.at[me], sums.at[me], sum_send.at[step - 1], sum_recv.at[step - 1], peer(step))
        for step in range(1, n)
    ]
    for copy in sum_copies:
        copy.start()
    cols = hot.shape[0]
    hot[...] = jnp.where(
        lax.broadcasted_iota(jnp.int32, (cols, n_obs), 0) == column_ref[...], 1.0, 0.0
    ).astype(bf16)
    for copy in sum_copies:
        copy.wait_recv()
    whole = sums[0]
    for m in range(1, n):
        whole = whole + sums[m]
    mean[...] = whole * (1.0 / members)

    for v in range(nv):
        for lane in range(lanes):
            flat = held.at[lane].reshape(block * nv, 128)
            picked = flat[pl.ds(v, block, stride=nv), :]
            across = pl.ds(lane * 128, 128)
            anom[v, span(me), across] = (picked - mean[pl.ds(v, 1), across]).astype(bf16)
    send(1)

    lift = 8
    for g in range(nv // lift):
        rows = anom[pl.ds(g * lift, lift), span(me), :].reshape(lift * block, cols)
        picked = mm(rows, hot[...])
        part = picked[:block] * weight_ref[pl.ds(g * lift, 1), :]
        for i in range(1, lift):
            part = part + picked[i * block : (i + 1) * block] * weight_ref[pl.ds(g * lift + i, 1), :]
        acc[...] = part if g == 0 else acc[...] + part
    seen[span(me), :] = acc[...].astype(bf16)
    send(0)
    send(2)

    mean_high, mean_low = split(mean[...])
    picked = mm(mean_high, hot[...]) + mm(mean_low, hot[...])
    seen_mean = jnp.sum(picked * weight_ref[...], axis=0, keepdims=True)
    own_row = lax.broadcasted_iota(jnp.int32, (n, 1), 0) == me
    my_rows = jnp.sum(jnp.where(own_row, rows_ref[...], 0), axis=0, keepdims=True)
    my_count = jnp.sum(jnp.where(own_row, count_ref[...], 0), axis=0, keepdims=True)
    live = lax.broadcasted_iota(jnp.int32, (1, n_set), 1) < my_count
    where = jnp.where(live, my_rows, -1)
    match = jnp.where(lax.broadcasted_iota(jnp.int32, (n_obs, n_set), 0) == where, 1.0, 0.0).astype(bf16)
    times = mm_t(jnp.ones((16, n_set), bf16), match)[:1]
    root = jnp.sqrt(times * rinv_ref[...])

    forward(0)
    send(3)
    send(4)
    arrive(0)
    forward(1)

    observed = seen[...].astype(f32)
    rest = jnp.mean(observed, axis=0, keepdims=True)
    scaled = split((observed - rest) * root)
    push = split((value_ref[...] - (seen_mean + rest)) * root)
    eye = jnp.where(
        lax.broadcasted_iota(jnp.int32, (members, members), 0)
        == lax.broadcasted_iota(jnp.int32, (members, members), 1),
        1.0,
        0.0,
    )
    cross = mm_t(scaled[0], scaled[1])
    posterior = (members - 1.0) * eye + (mm_t(scaled[0], scaled[0]) + (cross + mm_t(scaled[1], scaled[0])))
    wide = [jnp.broadcast_to(p, (16, n_obs)) for p in push]
    drive = mm_t(wide[0], scaled[0]) + (mm_t(wide[0], scaled[1]) + mm_t(wide[1], scaled[0]))
    square = jnp.sum(jnp.sum(posterior * posterior, axis=0, keepdims=True), axis=1, keepdims=True)
    norm = jnp.sqrt(square)
    iterate = posterior * (1.0 / norm)
    inverse = None
    for turn_index in range(NS_ITERS):
        step_whole = 1.5 * eye - 0.5 * iterate
        step_now = split(step_whole)
        if inverse is None:
            inverse = step_whole
        else:
            inverse = mm3(split(inverse), step_now)
        if turn_index < NS_ITERS - 1:
            iterate = mm3(split(mm3(split(iterate), step_now)), step_now)
        if turn_index == 2:
            forward(2)
    last = split(inverse)
    weight_row = mm3(split(mm3(split(drive), last)), last)[:1] * (1.0 / norm)
    turn[...] = (inverse * jnp.sqrt((members - 1.0) / norm) + weight_row).astype(bf16)
    turn_copies = [
        remote(
            turn.at[span(peer(step)), :],
            turns.at[span(me), :],
            turn_send.at[step - 1],
            turn_recv.at[step - 1],
            peer(step),
        )
        for step in range(1, n)
    ]
    for copy in turn_copies:
        copy.start()
    for part in range(5, CHUNKS + 1):
        send(part)
    turns[span(me), :] = turn[span(me), :]

    near = near_ref[...]
    share = interp_ref[...] / jnp.sum(interp_ref[...], axis=0, keepdims=True)
    point = [jnp.sum(jnp.where(near == m, share, 0.0), axis=0, keepdims=True) for m in range(n)]
    forward(3)
    for copy in turn_copies:
        copy.wait_recv()

    stores = []
    for part in range(1, CHUNKS + 1):
        if 3 < part + 1 <= CHUNKS:
            forward(part + 1)
        arrive(part)

        for v in range((part - 1) * group, part * group):
            product = mm(turns[...], anom[v])
            result = mean[pl.ds(v, 1), :] + product[:block] * point[0]
            for m in range(1, n):
                result = result + product[m * block : (m + 1) * block] * point[m]
            for lane in range(lanes):
                flat = result_held.at[lane].reshape(block * nv, 128)
                flat[pl.ds(v, block, stride=nv), :] = result[:, lane * 128 : (lane + 1) * 128]
        if part * group % 8 == 0:
            start_row = part * group // 8 * 8 - 8
            for lane in range(lanes):
                store = pltpu.make_async_copy(
                    result_held.at[lane, :, pl.ds(start_row, 8), :],
                    out_ref.at[:, pl.ds(start_row, 8), pl.ds(lane * 128, 128)],
                    result_sem.at[start_row // 8, lane],
                )
                store.start()
                stores.append(store)

    for copy in stores:
        copy.wait()
    for copy in sum_copies + turn_copies:
        copy.wait_send()
    for part in range(CHUNKS + 1):
        own_copy(part).wait_send()
        for step in range(1, chips):
            far_copy(part, step).wait_send()
            pass_copy(part, step).wait_send()


def local(
    ensemble,
    obs_weight,
    obs_value,
    obs_rinv,
    obs_column,
    set_rows,
    set_count,
    neighbour,
    interp_weight,
):
    n = lax.axis_size("member")
    block, nv, cols = ensemble.shape
    n_obs = obs_weight.shape[1]
    members = n * block
    far = max(n // 2 - 1, 1)
    parts = CHUNKS + 1
    dma = pltpu.SemaphoreType.DMA
    flops = 2 * members * members * nv * cols * n // 4 + 2 * block * nv * cols * n_obs
    return pl.pallas_call(
        functools.partial(kernel, n, block),
        out_shape=jax.ShapeDtypeStruct(ensemble.shape, f32),
        in_specs=[pl.BlockSpec(memory_space=pl.ANY)] + [pl.BlockSpec(memory_space=pltpu.VMEM)] * 8,
        out_specs=pl.BlockSpec(memory_space=pl.ANY),
        scratch_shapes=[
            pltpu.VMEM((cols // 128, block, nv, 128), f32),
            pltpu.VMEM((cols // 128, block, nv, 128), f32),
            pltpu.VMEM((n, nv, cols), f32),
            pltpu.VMEM((nv, cols), f32),
            pltpu.VMEM((nv, members, cols), bf16),
            pltpu.VMEM((members, n_obs), bf16),
            pltpu.VMEM((block, n_obs), f32),
            pltpu.VMEM((cols, n_obs), bf16),
            pltpu.VMEM((members, members), bf16),
            pltpu.VMEM((members, members), bf16),
            dma((n - 1,)),
            dma((n - 1,)),
            dma((n - 1,)),
            dma((n - 1,)),
            dma((parts,)),
            dma((parts,)),
            dma((parts, far)),
            dma((parts, far)),
            dma((parts, far)),
            dma((parts, far)),
            dma((cols // 128,)),
            dma((nv // 8, cols // 128)),
        ],
        compiler_params=pltpu.CompilerParams(
            collective_id=0, has_side_effects=True, vmem_limit_bytes=48 * 1024 * 1024
        ),
        cost_estimate=pl.CostEstimate(
            flops=flops, bytes_accessed=8 * block * nv * cols, transcendentals=0
        ),
    )(
        ensemble,
        obs_weight,
        obs_value.reshape(1, n_obs),
        obs_rinv.reshape(1, n_obs),
        obs_column.reshape(1, n_obs),
        set_rows,
        set_count.reshape(-1, 1),
        neighbour,
        interp_weight,
    )


def solution(mesh):
    placed = (
        P("member", None, "space"),
        P(None, "space"),
        P("space"),
        P("space"),
        P("space"),
        P("space", None),
        P("space"),
        P(None, "space"),
        P(None, "space"),
    )
    return jax.shard_map(
        local, mesh=mesh, in_specs=placed, out_specs=P("member", None, "space"), check_vma=False
    )
```

time: 131 us -> 48.4 us (0.37)
  blocking collectives: 47.5 us -> 0 us
  Pallas kernels: 0 us -> 39.3 us
  local copies, waits for them, and re-layouts: 40.1 us -> 8.68 us
  other arithmetic: 17.2 us -> 0 us
  matrix products: 14.6 us -> 0 us
  starting transfers between devices: 8.97 us -> 0 us
    pallas_call x0 -> x1, Pallas kernels: none -> 39.3 us  [local(): pl.pallas_call(functools.partial(kernel, n, block), out_shape=jax.ShapeDt...]
    all_to_all x1 -> x0, blocking collectives: 27.3 us -> none  [local(): lax.all_to_all(analysed, 'member', split_axis=0, concat_axis=1, tiled=True)]
    gather x5 -> x0, local copies, waits for them, and re-layouts: 25.8 us -> none  [the longest x1 14.6 us: local(): picked_vals = jnp.take(ensemble, obs_column, axis=2)]
    all_gather x1 -> x0, blocking collectives: 20.2 us -> none  [local(): everything = lax.all_gather(transform[None], 'member', axis=0, tiled=True)]
    dot_general x22 -> x0, matrix products: 14.6 us -> none  [the longest x4 7.16 us: contribution(): jnp.einsum('kl,kvc->lvc', matrix, anomalies, preferred_element_type=jnp.f...]
    reduce_sum x5 -> x0, other arithmetic: 10.1 us -> none  [the longest x1 8.27 us: local(): observed = jnp.sum(picked_vals * obs_weight[None], axis=1)]
    all_to_all x2 -> x0, starting transfers between devices: 8.97 us -> none  [the longest x1 4.68 us: local(): lax.all_to_all(ensemble, 'member', split_axis=1, concat_axis=0, tiled=True)]
    all_to_all x2 -> x0, local copies, waits for them, and re-layouts: 4.44 us -> none  [the longest x1 2.81 us: local(): lax.all_to_all(ensemble, 'member', split_axis=1, concat_axis=0, tiled=True)]
  transfers between devices with their start and end apart: 2 -> 0, of which waited for: 0 -> 0; matrix products, arithmetic and copies ran while one was open for 13% -> 0% of each run, Pallas kernels for 0% -> 0%
where the time goes in v1:
time: 48.4 us; the launch traced here: 48 us
  Pallas kernels  39.3 us (81%)
  local copies, waits for them, and re-layouts  8.68 us (18%)
    pallas_call x1, Pallas kernels, local(): pl.pallas_call(functools.partial(kernel, n, block), out_shape=jax.ShapeDt...  39.3 us
    unnamed x17, local copies, waits for them, and re-layouts  7.94 us

profile of v1, /device:TPU:1, one launch (start us, length us, event | category | flops | bytes accessed | tf_op | source)
XLA Modules:
  0.0 48.0 jit_solution(518944424257110155)
XLA Ops:
  0.0 0.7 %copy.10.count_ref = s32[4,1]{1,0:T(4,128)S(1)} copy(s32[4,1]{0,1:T(1,128)} %bitcast.7) | data formatting | bytes 32 | tf_op jit(solution)/shard_map/reshape | solution.py:362
  0.7 0.0 copy-start
  0.7 1.6 %copy-done = f32[64,32,256]{2,1,0:T(8,128)S(1)} copy-done((f32[64,32,256]{2,1,0:T(8,128)S(1)}, f32[64,32,256]{2,1,0:T(8,128)}, u32[]{:S(2)}) %copy-start) | copy-done | bytes 2097176
  2.3 0.0 copy-start.1
  2.3 0.9 %copy-done.1 = f32[32,1024]{1,0:T(8,128)S(1)} copy-done((f32[32,1024]{1,0:T(8,128)S(1)}, f32[32,1024]{1,0:T(8,128)}, u32[]{:S(2)}) %copy-start.1) | copy-done | bytes 131096
  3.2 0.0 copy-start.2
  3.2 0.7 %copy-done.2 = s32[4,512]{1,0:T(4,128)S(1)} copy-done((s32[4,512]{1,0:T(4,128)S(1)}, s32[4,512]{1,0:T(4,128)}, u32[]{:S(2)}) %copy-start.2) | copy-done | bytes 8216
  3.9 0.0 copy-start.3
  3.9 0.7 %copy-done.3 = f32[1024]{0:T(1024)S(1)} copy-done((f32[1024]{0:T(1024)S(1)}, f32[1024]{0:T(1024)}, u32[]{:S(2)}) %copy-start.3) | copy-done | bytes 4120
  4.6 0.0 copy-start.4
  4.6 0.7 %copy-done.4 = f32[1024]{0:T(1024)S(1)} copy-done((f32[1024]{0:T(1024)S(1)}, f32[1024]{0:T(1024)}, u32[]{:S(2)}) %copy-start.4) | copy-done | bytes 4120
  5.3 0.0 copy-start.5
  5.3 0.7 %copy-done.5 = s32[1024]{0:T(1024)S(1)} copy-done((s32[1024]{0:T(1024)S(1)}, s32[1024]{0:T(1024)}, u32[]{:S(2)}) %copy-start.5) | copy-done | bytes 4120
  6.0 0.0 copy-start.6
  6.0 0.7 %copy-done.6 = s32[4,256]{1,0:T(4,128)S(1)} copy-done((s32[4,256]{1,0:T(4,128)S(1)}, s32[4,256]{1,0:T(4,128)}, u32[]{:S(2)}) %copy-start.6) | copy-done | bytes 4120
  6.7 0.0 copy-start.7
  6.7 0.7 %copy-done.7 = f32[4,256]{1,0:T(4,128)S(1)} copy-done((f32[4,256]{1,0:T(4,128)S(1)}, f32[4,256]{1,0:T(4,128)}, u32[]{:S(2)}) %copy-start.7) | copy-done | bytes 4120
  7.4 39.3 %shard_map.91 = f32[64,32,256]{2,1,0:T(8,128)S(1)} custom-call(f32[64,32,256]{2,1,0:T(8,128)S(1)} %copy-done, f32[32,1024]{1,0:T(8,128)S(1)} %copy-done.1, f32[1,1024]{1,0:T(1,128)S(1)} %bitcast.4, f32[1,1024]{1,0:T(1,128)S(1)} %bitcast.5, s32[1,1024]{1,0:T(1,128)S(1)} %bitcast.6, s32[4,512]{1,0:T(4,128)S(1)} %copy-done.2, s32[4,1]{1,0:T(4,128)S(1)} %copy.10.count_ref, ...), custom_call_target="tpu_custom_call" | custom-call | flops 2147483648 | bytes 4194304 | tf_op jit(solution)/shard_map/pallas_call | solution.py:320
  46.7 1.3 %copy.12 = f32[64,32,256]{2,1,0:T(8,128)} copy(f32[64,32,256]{2,1,0:T(8,128)S(1)} %shard_map.91) | data formatting | bytes 4194304
Async XLA Ops:
  0.7 1.6 %copy-start = (f32[64,32,256]{2,1,0:T(8,128)S(1)}, f32[64,32,256]{2,1,0:T(8,128)}, u32[]{:S(2)}) copy-start(f32[64,32,256]{2,1,0:T(8,128)} %ens_ref.1) | copy-start | bytes 6291460
  2.3 0.9 %copy-start.1 = (f32[32,1024]{1,0:T(8,128)S(1)}, f32[32,1024]{1,0:T(8,128)}, u32[]{:S(2)}) copy-start(f32[32,1024]{1,0:T(8,128)} %weight_ref.1) | copy-start | bytes 393220
  3.2 0.7 %copy-start.2 = (s32[4,512]{1,0:T(4,128)S(1)}, s32[4,512]{1,0:T(4,128)}, u32[]{:S(2)}) copy-start(s32[4,512]{1,0:T(4,128)} %rows_ref.1) | copy-start | bytes 24580
  3.9 0.7 %copy-start.3 = (f32[1024]{0:T(1024)S(1)}, f32[1024]{0:T(1024)}, u32[]{:S(2)}) copy-start(f32[1024]{0:T(1024)} %param.11) | copy-start | bytes 12292
  4.6 0.7 %copy-start.4 = (f32[1024]{0:T(1024)S(1)}, f32[1024]{0:T(1024)}, u32[]{:S(2)}) copy-start(f32[1024]{0:T(1024)} %param.12) | copy-start | bytes 12292
  5.3 0.7 %copy-start.5 = (s32[1024]{0:T(1024)S(1)}, s32[1024]{0:T(1024)}, u32[]{:S(2)}) copy-start(s32[1024]{0:T(1024)} %param.13) | copy-start | bytes 12292
  6.0 0.7 %copy-start.6 = (s32[4,256]{1,0:T(4,128)S(1)}, s32[4,256]{1,0:T(4,128)}, u32[]{:S(2)}) copy-start(s32[4,256]{1,0:T(4,128)} %near_ref.1) | copy-start | bytes 12292
  6.7 0.7 %copy-start.7 = (f32[4,256]{1,0:T(4,128)S(1)}, f32[4,256]{1,0:T(4,128)}, u32[]{:S(2)}) copy-start(f32[4,256]{1,0:T(4,128)} %interp_ref.1) | copy-start | bytes 12292

commit v2 on v1

--- a/solution.py
+++ b/solution.py
@@ -9,6 +9,7 @@
 
 NS_ITERS = 5
 CHUNKS = 8
+EARLY = 1
 MESH = pl.DeviceIdType.MESH
 f32 = jnp.float32
 bf16 = jnp.bfloat16
@@ -35,14 +36,14 @@
     n,
     block,
     ens_ref,
-    weight_ref,
-    value_ref,
-    rinv_ref,
-    column_ref,
-    rows_ref,
-    count_ref,
-    near_ref,
-    interp_ref,
+    weight_in,
+    value_in,
+    rinv_in,
+    column_in,
+    rows_in,
+    count_in,
+    near_in,
+    interp_in,
     out_ref,
     held,
     result_held,
@@ -66,6 +67,18 @@
     pass_recv,
     held_sem,
     result_sem,
+    loose,
+    shift,
+    lean,
+    weight_ref,
+    value_ref,
+    rinv_ref,
+    column_ref,
+    rows_ref,
+    count_ref,
+    near_ref,
+    interp_ref,
+    in_sem,
 ):
     me = lax.axis_index("member")
     chips = n // 2
@@ -74,8 +87,8 @@
     nv = mean.shape[0]
     members = n * block
     group = nv // CHUNKS
-    n_obs = weight_ref.shape[1]
-    n_set = rows_ref.shape[1]
+    n_obs = weight_in.shape[1]
+    n_set = rows_in.shape[1]
 
     def peer(step):
         return lax.rem(me + step, n)
@@ -106,13 +119,27 @@
         )
         for lane in range(lanes)
     ]
-    for copy in loads:
+    small = [
+        pltpu.make_async_copy(src, dst, in_sem.at[i])
+        for i, (src, dst) in enumerate(
+            (
+                (column_in, column_ref),
+                (weight_in, weight_ref),
+                (value_in, value_ref),
+                (rinv_in, rinv_ref),
+                (rows_in, rows_ref),
+                (count_in, count_ref),
+                (near_in, near_ref),
+                (interp_in, interp_ref),
+            )
+        )
+    ]
+    for copy in loads + small:
         copy.start()
 
     barrier = pltpu.get_barrier_semaphore()
     for step in range(1, n):
         pl.semaphore_signal(barrier, inc=1, device_id={"member": peer(step)}, device_id_type=MESH)
-    pl.semaphore_wait(barrier, n - 1)
 
     def view(part, index):
         if part == 0:
@@ -145,6 +172,13 @@
         own_copy(part).wait_recv()
         for step in range(1, chips):
             pass_copy(part, step).wait_recv()
+
+    def centre(v, about, into, rows):
+        for lane in range(lanes):
+            flat = held.at[lane].reshape(block * nv, 128)
+            picked = flat[pl.ds(v, block, stride=nv), :]
+            across = pl.ds(lane * 128, 128)
+            into[v, rows, across] = (picked - about[v : v + 1, lane * 128 : (lane + 1) * 128]).astype(bf16)
 
     for lane in range(lanes):
         loads[lane].wait()
@@ -152,34 +186,30 @@
         for k in range(1, block):
             total = total + held[lane, k]
         sums[me, :, pl.ds(lane * 128, 128)] = total
+    own_mean = sums[me] * (1.0 / block)
+    for v in range(EARLY * group):
+        centre(v, own_mean, anom, span(me))
+    pl.semaphore_wait(barrier, n - 1)
     sum_copies = [
         remote(sums.at[me], sums.at[me], sum_send.at[step - 1], sum_recv.at[step - 1], peer(step))
         for step in range(1, n)
     ]
     for copy in sum_copies:
         copy.start()
+    for part in range(1, EARLY + 1):
+        send(part)
+    for v in range(nv):
+        centre(v, own_mean, loose, pl.ds(0, block))
+    for copy in small:
+        copy.wait()
     cols = hot.shape[0]
     hot[...] = jnp.where(
         lax.broadcasted_iota(jnp.int32, (cols, n_obs), 0) == column_ref[...], 1.0, 0.0
     ).astype(bf16)
-    for copy in sum_copies:
-        copy.wait_recv()
-    whole = sums[0]
-    for m in range(1, n):
-        whole = whole + sums[m]
-    mean[...] = whole * (1.0 / members)
-
-    for v in range(nv):
-        for lane in range(lanes):
-            flat = held.at[lane].reshape(block * nv, 128)
-            picked = flat[pl.ds(v, block, stride=nv), :]
-            across = pl.ds(lane * 128, 128)
-            anom[v, span(me), across] = (picked - mean[pl.ds(v, 1), across]).astype(bf16)
-    send(1)
 
     lift = 8
     for g in range(nv // lift):
-        rows = anom[pl.ds(g * lift, lift), span(me), :].reshape(lift * block, cols)
+        rows = loose[pl.ds(g * lift, lift), :, :].reshape(lift * block, cols)
         picked = mm(rows, hot[...])
         part = picked[:block] * weight_ref[pl.ds(g * lift, 1), :]
         for i in range(1, lift):
@@ -187,14 +217,30 @@
         acc[...] = part if g == 0 else acc[...] + part
     seen[span(me), :] = acc[...].astype(bf16)
     send(0)
-    send(2)
-
-    mean_high, mean_low = split(mean[...])
-    picked = mm(mean_high, hot[...]) + mm(mean_low, hot[...])
-    seen_mean = jnp.sum(picked * weight_ref[...], axis=0, keepdims=True)
+
+    for copy in sum_copies:
+        copy.wait_recv()
+    whole = sums[0]
+    for m in range(1, n):
+        whole = whole + sums[m]
+    mean[...] = whole * (1.0 / members)
+    middle = mean[...]
+    for m in range(n):
+        shift[m] = sums[m] * (1.0 / block) - middle
+    for v in range(EARLY * group, nv):
+        centre(v, middle, anom, span(me))
+        if (v + 1) % group == 0 and (v + 1) // group <= EARLY + 2:
+            send((v + 1) // group)
+
+    seen_parts = []
+    for m in range(n + 1):
+        high, low = split(middle if m == n else shift[m])
+        picked = mm(high, hot[...]) + mm(low, hot[...])
+        seen_parts.append(jnp.sum(picked * weight_ref[...], axis=0, keepdims=True))
     own_row = lax.broadcasted_iota(jnp.int32, (n, 1), 0) == me
     my_rows = jnp.sum(jnp.where(own_row, rows_ref[...], 0), axis=0, keepdims=True)
-    my_count = jnp.sum(jnp.where(own_row, count_ref[...], 0), axis=0, keepdims=True)
+    own_lane = lax.broadcasted_iota(jnp.int32, (1, n), 1) == me
+    my_count = jnp.sum(jnp.where(own_lane, count_ref[...], 0), axis=1, keepdims=True)
     live = lax.broadcasted_iota(jnp.int32, (1, n_set), 1) < my_count
     where = jnp.where(live, my_rows, -1)
     match = jnp.where(lax.broadcasted_iota(jnp.int32, (n_obs, n_set), 0) == where, 1.0, 0.0).astype(bf16)
@@ -202,15 +248,16 @@
     root = jnp.sqrt(times * rinv_ref[...])
 
     forward(0)
-    send(3)
-    send(4)
+    forward(1)
+    send(EARLY + 3)
     arrive(0)
-    forward(1)
-
-    observed = seen[...].astype(f32)
+
+    observed = jnp.concatenate(
+        [seen[pl.ds(m * block, block), :].astype(f32) + seen_parts[m] for m in range(n)], axis=0
+    )
     rest = jnp.mean(observed, axis=0, keepdims=True)
     scaled = split((observed - rest) * root)
-    push = split((value_ref[...] - (seen_mean + rest)) * root)
+    push = split((value_ref[...] - (seen_parts[n] + rest)) * root)
     eye = jnp.where(
         lax.broadcasted_iota(jnp.int32, (members, members), 0)
         == lax.broadcasted_iota(jnp.int32, (members, members), 1),
@@ -234,8 +281,12 @@
             inverse = mm3(split(inverse), step_now)
         if turn_index < NS_ITERS - 1:
             iterate = mm3(split(mm3(split(iterate), step_now)), step_now)
-        if turn_index == 2:
+        if turn_index == 1:
+            send(EARLY + 4)
             forward(2)
+        if turn_index == 3:
+            send(EARLY + 5)
+            forward(3)
     last = split(inverse)
     weight_row = mm3(split(mm3(split(drive), last)), last)[:1] * (1.0 / norm)
     turn[...] = (inverse * jnp.sqrt((members - 1.0) / norm) + weight_row).astype(bf16)
@@ -251,20 +302,34 @@
     ]
     for copy in turn_copies:
         copy.start()
-    for part in range(5, CHUNKS + 1):
+    for part in range(EARLY + 6, CHUNKS + 1):
         send(part)
     turns[span(me), :] = turn[span(me), :]
 
     near = near_ref[...]
     share = interp_ref[...] / jnp.sum(interp_ref[...], axis=0, keepdims=True)
     point = [jnp.sum(jnp.where(near == m, share, 0.0), axis=0, keepdims=True) for m in range(n)]
-    forward(3)
+    forward(4)
     for copy in turn_copies:
         copy.wait_recv()
+    for m in range(n):
+        block_sums = [
+            jnp.sum(
+                turns[pl.ds(j * block, block), pl.ds(0, members)].astype(f32)
+                * jnp.where(lax.broadcasted_iota(jnp.int32, (1, members), 1) // block == m, 1.0, 0.0),
+                axis=1,
+                keepdims=True,
+            )
+            for j in range(n)
+        ]
+        gathered = block_sums[0] * point[0]
+        for j in range(1, n):
+            gathered = gathered + block_sums[j] * point[j]
+        lean[m] = gathered
 
     stores = []
     for part in range(1, CHUNKS + 1):
-        if 3 < part + 1 <= CHUNKS:
+        if 4 < part + 1 <= CHUNKS:
             forward(part + 1)
         arrive(part)
 
@@ -273,6 +338,9 @@
             result = mean[pl.ds(v, 1), :] + product[:block] * point[0]
             for m in range(1, n):
                 result = result + product[m * block : (m + 1) * block] * point[m]
+            if part <= EARLY:
+                for m in range(n):
+                    result = result + lean[m] * shift[m, pl.ds(v, 1), :]
             for lane in range(lanes):
                 flat = result_held.at[lane].reshape(block * nv, 128)
                 flat[pl.ds(v, block, stride=nv), :] = result[:, lane * 128 : (lane + 1) * 128]
@@ -320,7 +388,7 @@
     return pl.pallas_call(
         functools.partial(kernel, n, block),
         out_shape=jax.ShapeDtypeStruct(ensemble.shape, f32),
-        in_specs=[pl.BlockSpec(memory_space=pl.ANY)] + [pl.BlockSpec(memory_space=pltpu.VMEM)] * 8,
+        in_specs=[pl.BlockSpec(memory_space=pltpu.HBM)] * 9,
         out_specs=pl.BlockSpec(memory_space=pl.ANY),
         scratch_shapes=[
             pltpu.VMEM((cols // 128, block, nv, 128), f32),
@@ -345,9 +413,21 @@
             dma((parts, far)),
             dma((cols // 128,)),
             dma((nv // 8, cols // 128)),
+            pltpu.VMEM((nv, block, cols), bf16),
+            pltpu.VMEM((n, nv, cols), f32),
+            pltpu.VMEM((n, block, cols), f32),
+            pltpu.VMEM((nv, n_obs), f32),
+            pltpu.VMEM((1, n_obs), f32),
+            pltpu.VMEM((1, n_obs), f32),
+            pltpu.VMEM((1, n_obs), jnp.int32),
+            pltpu.VMEM(set_rows.shape, jnp.int32),
+            pltpu.VMEM((1, n), jnp.int32),
+            pltpu.VMEM(neighbour.shape, jnp.int32),
+            pltpu.VMEM(interp_weight.shape, f32),
+            dma((8,)),
         ],
         compiler_params=pltpu.CompilerParams(
-            collective_id=0, has_side_effects=True, vmem_limit_bytes=48 * 1024 * 1024
+            collective_id=0, has_side_effects=True, vmem_limit_bytes=60 * 1024 * 1024
         ),
         cost_estimate=pl.CostEstimate(
             flops=flops, bytes_accessed=8 * block * nv * cols, transcendentals=0
@@ -359,7 +439,7 @@
         obs_rinv.reshape(1, n_obs),
         obs_column.reshape(1, n_obs),
         set_rows,
-        set_count.reshape(-1, 1),
+        set_count.reshape(1, n),
         neighbour,
         interp_weight,
     )

time: 48.4 us -> 40.1 us (0.83)
  local copies, waits for them, and re-layouts: 8.68 us -> 3.16 us
  Pallas kernels: 39.3 us -> 36.8 us
    unnamed x17 -> x1, local copies, waits for them, and re-layouts: 7.94 us -> 3.16 us
    pallas_call x1, Pallas kernels: 39.3 us -> 36.8 us  [local(): pl.pallas_call(functools.partial(kernel, n, block), out_shape=jax.ShapeDt...]
    reshape x1 -> x0, local copies, waits for them, and re-layouts: 0.74 us -> none  [local(): set_count.reshape(-1, 1)]
where the time goes in v2:
time: 40.1 us; the launch traced here: 39.9 us
  Pallas kernels  36.8 us (92%)
  local copies, waits for them, and re-layouts  3.16 us (8%)
    pallas_call x1, Pallas kernels, local(): pl.pallas_call(functools.partial(kernel, n, block), out_shape=jax.ShapeDt...  36.8 us
    unnamed x1, local copies, waits for them, and re-layouts  3.16 us

profile of v2, /device:TPU:1, one launch (start us, length us, event | category | flops | bytes accessed | tf_op | source)
XLA Modules:
  0.0 39.9 jit_solution(9248136766894015596)
XLA Ops:
  0.0 36.8 %shard_map.91 = f32[64,32,256]{2,1,0:T(8,128)} custom-call(f32[64,32,256]{2,1,0:T(8,128)} %ens_ref.1, f32[32,1024]{1,0:T(8,128)} %weight_in.1, f32[1,1024]{1,0:T(1,128)} %bitcast.4, f32[1,1024]{1,0:T(1,128)} %bitcast.5, s32[1,1024]{1,0:T(1,128)} %bitcast.6, s32[4,512]{1,0:T(4,128)} %rows_in.1, s32[1,4]{1,0:T(1,128)} %bitcast.7, s32[4,256]{1,0:T(4,128)} %near_in.1, ...), custom_call_target="tpu_custom_call" | custom-call | flops 2147483648 | bytes 4194304 | tf_op jit(solution)/shard_map/pallas_call | solution.py:388
  36.8 3.2 %copy.11 = f32[64,32,256]{2,1,0:T(8,128)} copy(f32[64,32,256]{2,1,0:T(8,128)} %shard_map.91) | data formatting | bytes 4194304

commit v3 on v2

--- a/solution.py
+++ b/solution.py
@@ -231,12 +231,15 @@
         centre(v, middle, anom, span(me))
         if (v + 1) % group == 0 and (v + 1) // group <= EARLY + 2:
             send((v + 1) // group)
-
+    forward(0)
+    send(EARLY + 3)
+
+    high, low = split(jnp.concatenate([shift[m] for m in range(n)] + [middle], axis=0))
+    picked = mm(jnp.concatenate([high, low], axis=0), hot[...])
     seen_parts = []
     for m in range(n + 1):
-        high, low = split(middle if m == n else shift[m])
-        picked = mm(high, hot[...]) + mm(low, hot[...])
-        seen_parts.append(jnp.sum(picked * weight_ref[...], axis=0, keepdims=True))
+        both = picked[m * nv : (m + 1) * nv] + picked[(n + 1 + m) * nv : (n + 2 + m) * nv]
+        seen_parts.append(jnp.sum(both * weight_ref[...], axis=0, keepdims=True))
     own_row = lax.broadcasted_iota(jnp.int32, (n, 1), 0) == me
     my_rows = jnp.sum(jnp.where(own_row, rows_ref[...], 0), axis=0, keepdims=True)
     own_lane = lax.broadcasted_iota(jnp.int32, (1, n), 1) == me
@@ -247,10 +250,9 @@
     times = mm_t(jnp.ones((16, n_set), bf16), match)[:1]
     root = jnp.sqrt(times * rinv_ref[...])
 
-    forward(0)
+    arrive(0)
     forward(1)
-    send(EARLY + 3)
-    arrive(0)
+    send(EARLY + 4)
 
     observed = jnp.concatenate(
         [seen[pl.ds(m * block, block), :].astype(f32) + seen_parts[m] for m in range(n)], axis=0
@@ -264,10 +266,12 @@
         1.0,
         0.0,
     )
-    cross = mm_t(scaled[0], scaled[1])
-    posterior = (members - 1.0) * eye + (mm_t(scaled[0], scaled[0]) + (cross + mm_t(scaled[1], scaled[0])))
-    wide = [jnp.broadcast_to(p, (16, n_obs)) for p in push]
-    drive = mm_t(wide[0], scaled[0]) + (mm_t(wide[0], scaled[1]) + mm_t(wide[1], scaled[0]))
+    left = [
+        jnp.concatenate([scaled[i], jnp.broadcast_to(push[i], (16, n_obs))], axis=0) for i in range(2)
+    ]
+    grown = mm_t(left[0], scaled[0]) + (mm_t(left[0], scaled[1]) + mm_t(left[1], scaled[0]))
+    posterior = (members - 1.0) * eye + grown[:members]
+    drive = grown[members:]
     square = jnp.sum(jnp.sum(posterior * posterior, axis=0, keepdims=True), axis=1, keepdims=True)
     norm = jnp.sqrt(square)
     iterate = posterior * (1.0 / norm)
@@ -275,17 +279,26 @@
     for turn_index in range(NS_ITERS):
         step_whole = 1.5 * eye - 0.5 * iterate
         step_now = split(step_whole)
+        final = turn_index == NS_ITERS - 1
         if inverse is None:
             inverse = step_whole
+            if not final:
+                iterate = mm3(split(iterate), step_now)
+        elif final:
+            inverse = mm3(split(inverse), step_now)
         else:
-            inverse = mm3(split(inverse), step_now)
-        if turn_index < NS_ITERS - 1:
-            iterate = mm3(split(mm3(split(iterate), step_now)), step_now)
+            both = mm3(split(jnp.concatenate([iterate, inverse], axis=0)), step_now)
+            iterate = both[:members]
+            inverse = both[members:]
+        if not final:
+            iterate = mm3(split(iterate), step_now)
+        if turn_index == 0:
+            send(EARLY + 5)
         if turn_index == 1:
-            send(EARLY + 4)
             forward(2)
+        if turn_index == 2:
+            send(EARLY + 6)
         if turn_index == 3:
-            send(EARLY + 5)
             forward(3)
     last = split(inverse)
     weight_row = mm3(split(mm3(split(drive), last)), last)[:1] * (1.0 / norm)
@@ -302,7 +315,7 @@
     ]
     for copy in turn_copies:
         copy.start()
-    for part in range(EARLY + 6, CHUNKS + 1):
+    for part in range(EARLY + 7, CHUNKS + 1):
         send(part)
     turns[span(me), :] = turn[span(me), :]
 
@@ -427,21 +440,26 @@
             dma((8,)),
         ],
         compiler_params=pltpu.CompilerParams(
-            collective_id=0, has_side_effects=True, vmem_limit_bytes=60 * 1024 * 1024
+            collective_id=0, has_side_effects=True, vmem_limit_bytes=48 * 1024 * 1024
         ),
         cost_estimate=pl.CostEstimate(
             flops=flops, bytes_accessed=8 * block * nv * cols, transcendentals=0
         ),
     )(
-        ensemble,
-        obs_weight,
-        obs_value.reshape(1, n_obs),
-        obs_rinv.reshape(1, n_obs),
-        obs_column.reshape(1, n_obs),
-        set_rows,
-        set_count.reshape(1, n),
-        neighbour,
-        interp_weight,
+        *[
+            pltpu.with_memory_space_constraint(operand, pltpu.HBM)
+            for operand in (
+                ensemble,
+                obs_weight,
+                obs_value.reshape(1, n_obs),
+                obs_rinv.reshape(1, n_obs),
+                obs_column.reshape(1, n_obs),
+                set_rows,
+                set_count.reshape(1, n),
+                neighbour,
+                interp_weight,
+            )
+        ]
     )
 
 

time: 40.1 us -> 39.2 us (0.978)
  local copies, waits for them, and re-layouts: 3.16 us -> 1.32 us
  Pallas kernels: 36.8 us -> 37.7 us
    unnamed x1, local copies, waits for them, and re-layouts: 3.16 us -> 1.32 us
    pallas_call x1, Pallas kernels: 36.8 us -> 37.7 us  [local(): pl.pallas_call(functools.partial(kernel, n, block), out_shape=jax.ShapeDt...]
where the time goes in v3:
time: 39.2 us; the launch traced here: 39.1 us
  Pallas kernels  37.7 us (96%)
  local copies, waits for them, and re-layouts  1.32 us (3%)
    pallas_call x1, Pallas kernels, local(): pl.pallas_call(functools.partial(kernel, n, block), out_shape=jax.ShapeDt...  37.7 us
    unnamed x1, local copies, waits for them, and re-layouts  1.32 us

profile of v3, /device:TPU:1, one launch (start us, length us, event | category | flops | bytes accessed | tf_op | source)
XLA Modules:
  0.0 39.1 jit_solution(1128806852126700242)
XLA Ops:
  0.0 37.7 %shard_map.91 = f32[64,32,256]{2,1,0:T(8,128)S(1)} custom-call(f32[64,32,256]{2,1,0:T(8,128)} %ens_ref.1, f32[32,1024]{1,0:T(8,128)} %weight_in.1, f32[1,1024]{1,0:T(1,128)} %bitcast.4, f32[1,1024]{1,0:T(1,128)} %bitcast.5, s32[1,1024]{1,0:T(1,128)} %bitcast.6, s32[4,512]{1,0:T(4,128)} %rows_in.1, s32[1,4]{1,0:T(1,128)} %bitcast.7, s32[4,256]{1,0:T(4,128)} %near_in.1, ...), custom_call_target="tpu_custom_call" | custom-call | flops 2147483648 | bytes 4194304 | tf_op jit(solution)/shard_map/pallas_call | solution.py:401
  37.8 1.3 %copy.11 = f32[64,32,256]{2,1,0:T(8,128)} copy(f32[64,32,256]{2,1,0:T(8,128)S(1)} %shard_map.91) | data formatting | bytes 4194304

commit v4 on v3

--- a/solution.py
+++ b/solution.py
@@ -55,8 +55,6 @@
     hot,
     turn,
     turns,
-    sum_send,
-    sum_recv,
     turn_send,
     turn_recv,
     own_send,
@@ -144,6 +142,8 @@
     def view(part, index):
         if part == 0:
             return seen.at[span(index), :]
+        if part == CHUNKS + 1:
+            return sums.at[index]
         return anom.at[pl.ds((part - 1) * group, group), span(index), :]
 
     def own_copy(part):
@@ -190,12 +190,7 @@
     for v in range(EARLY * group):
         centre(v, own_mean, anom, span(me))
     pl.semaphore_wait(barrier, n - 1)
-    sum_copies = [
-        remote(sums.at[me], sums.at[me], sum_send.at[step - 1], sum_recv.at[step - 1], peer(step))
-        for step in range(1, n)
-    ]
-    for copy in sum_copies:
-        copy.start()
+    send(CHUNKS + 1)
     for part in range(1, EARLY + 1):
         send(part)
     for v in range(nv):
@@ -207,6 +202,7 @@
         lax.broadcasted_iota(jnp.int32, (cols, n_obs), 0) == column_ref[...], 1.0, 0.0
     ).astype(bf16)
 
+    forward(CHUNKS + 1)
     lift = 8
     for g in range(nv // lift):
         rows = loose[pl.ds(g * lift, lift), :, :].reshape(lift * block, cols)
@@ -218,8 +214,7 @@
     seen[span(me), :] = acc[...].astype(bf16)
     send(0)
 
-    for copy in sum_copies:
-        copy.wait_recv()
+    arrive(CHUNKS + 1)
     whole = sums[0]
     for m in range(1, n):
         whole = whole + sums[m]
@@ -232,7 +227,6 @@
         if (v + 1) % group == 0 and (v + 1) // group <= EARLY + 2:
             send((v + 1) // group)
     forward(0)
-    send(EARLY + 3)
 
     high, low = split(jnp.concatenate([shift[m] for m in range(n)] + [middle], axis=0))
     picked = mm(jnp.concatenate([high, low], axis=0), hot[...])
@@ -252,7 +246,7 @@
 
     arrive(0)
     forward(1)
-    send(EARLY + 4)
+    send(EARLY + 3)
 
     observed = jnp.concatenate(
         [seen[pl.ds(m * block, block), :].astype(f32) + seen_parts[m] for m in range(n)], axis=0
@@ -292,12 +286,11 @@
             inverse = both[members:]
         if not final:
             iterate = mm3(split(iterate), step_now)
-        if turn_index == 0:
+        if turn_index == 1:
+            send(EARLY + 4)
+            forward(2)
+        if turn_index == 3:
             send(EARLY + 5)
-        if turn_index == 1:
-            forward(2)
-        if turn_index == 2:
-            send(EARLY + 6)
         if turn_index == 3:
             forward(3)
     last = split(inverse)
@@ -315,7 +308,7 @@
     ]
     for copy in turn_copies:
         copy.start()
-    for part in range(EARLY + 7, CHUNKS + 1):
+    for part in range(EARLY + 6, CHUNKS + 1):
         send(part)
     turns[span(me), :] = turn[span(me), :]
 
@@ -346,8 +339,11 @@
             forward(part + 1)
         arrive(part)
 
-        for v in range((part - 1) * group, part * group):
-            product = mm(turns[...], anom[v])
+        first = (part - 1) * group
+        wide = mm(turns[...], jnp.concatenate([anom[first + i] for i in range(group)], axis=1))
+        for i in range(group):
+            v = first + i
+            product = wide[:, i * cols : (i + 1) * cols]
             result = mean[pl.ds(v, 1), :] + product[:block] * point[0]
             for m in range(1, n):
                 result = result + product[m * block : (m + 1) * block] * point[m]
@@ -370,9 +366,9 @@
 
     for copy in stores:
         copy.wait()
-    for copy in sum_copies + turn_copies:
+    for copy in turn_copies:
         copy.wait_send()
-    for part in range(CHUNKS + 1):
+    for part in range(CHUNKS + 2):
         own_copy(part).wait_send()
         for step in range(1, chips):
             far_copy(part, step).wait_send()
@@ -395,7 +391,7 @@
     n_obs = obs_weight.shape[1]
     members = n * block
     far = max(n // 2 - 1, 1)
-    parts = CHUNKS + 1
+    parts = CHUNKS + 2
     dma = pltpu.SemaphoreType.DMA
     flops = 2 * members * members * nv * cols * n // 4 + 2 * block * nv * cols * n_obs
     return pl.pallas_call(
@@ -414,8 +410,6 @@
             pltpu.VMEM((cols, n_obs), bf16),
             pltpu.VMEM((members, members), bf16),
             pltpu.VMEM((members, members), bf16),
-            dma((n - 1,)),
-            dma((n - 1,)),
             dma((n - 1,)),
             dma((n - 1,)),
             dma((parts,)),

time: 39.2 us -> 36.8 us (0.939)
  Pallas kernels: 37.7 us -> 35.4 us
    pallas_call x1, Pallas kernels: 37.7 us -> 35.4 us  [local(): pl.pallas_call(functools.partial(kernel, n, block), out_shape=jax.ShapeDt...]
where the time goes in v4:
time: 36.8 us; the launch traced here: 36.7 us
  Pallas kernels  35.4 us (96%)
  local copies, waits for them, and re-layouts  1.32 us (4%)
    pallas_call x1, Pallas kernels, local(): pl.pallas_call(functools.partial(kernel, n, block), out_shape=jax.ShapeDt...  35.4 us
    unnamed x1, local copies, waits for them, and re-layouts  1.32 us

profile of v4, /device:TPU:1, one launch (start us, length us, event | category | flops | bytes accessed | tf_op | source)
XLA Modules:
  0.0 36.7 jit_solution(126647786512943724)
XLA Ops:
  0.0 35.4 %shard_map.91 = f32[64,32,256]{2,1,0:T(8,128)S(1)} custom-call(f32[64,32,256]{2,1,0:T(8,128)} %ens_ref.1, f32[32,1024]{1,0:T(8,128)} %weight_in.1, f32[1,1024]{1,0:T(1,128)} %bitcast.4, f32[1,1024]{1,0:T(1,128)} %bitcast.5, s32[1,1024]{1,0:T(1,128)} %bitcast.6, s32[4,512]{1,0:T(4,128)} %rows_in.1, s32[1,4]{1,0:T(1,128)} %bitcast.7, s32[4,256]{1,0:T(4,128)} %near_in.1, ...), custom_call_target="tpu_custom_call" | custom-call | flops 2147483648 | bytes 4194304 | tf_op jit(solution)/shard_map/pallas_call | solution.py:397
  35.4 1.3 %copy.11 = f32[64,32,256]{2,1,0:T(8,128)} copy(f32[64,32,256]{2,1,0:T(8,128)S(1)} %shard_map.91) | data formatting | bytes 4194304

commit v5 on v4

--- a/solution.py
+++ b/solution.py
@@ -222,10 +222,13 @@
     middle = mean[...]
     for m in range(n):
         shift[m] = sums[m] * (1.0 / block) - middle
-    for v in range(EARLY * group, nv):
-        centre(v, middle, anom, span(me))
-        if (v + 1) % group == 0 and (v + 1) // group <= EARLY + 2:
-            send((v + 1) // group)
+    def centre_part(part):
+        for v in range((part - 1) * group, part * group):
+            centre(v, middle, anom, span(me))
+
+    for part in range(EARLY + 1, EARLY + 3):
+        centre_part(part)
+        send(part)
     forward(0)
 
     high, low = split(jnp.concatenate([shift[m] for m in range(n)] + [middle], axis=0))
@@ -244,6 +247,7 @@
     times = mm_t(jnp.ones((16, n_set), bf16), match)[:1]
     root = jnp.sqrt(times * rinv_ref[...])
 
+    centre_part(EARLY + 3)
     arrive(0)
     forward(1)
     send(EARLY + 3)
@@ -274,6 +278,8 @@
         step_whole = 1.5 * eye - 0.5 * iterate
         step_now = split(step_whole)
         final = turn_index == NS_ITERS - 1
+        if EARLY + 4 + turn_index <= CHUNKS:
+            centre_part(EARLY + 4 + turn_index)
         if inverse is None:
             inverse = step_whole
             if not final:

time: 36.8 us -> 36.8 us (level)
  no operation moved by 1% of the time
where the time goes in v5:
time: 36.8 us; the launch traced here: 36.7 us
  Pallas kernels  35.4 us (96%)
  local copies, waits for them, and re-layouts  1.32 us (4%)
    pallas_call x1, Pallas kernels, local(): pl.pallas_call(functools.partial(kernel, n, block), out_shape=jax.ShapeDt...  35.4 us
    unnamed x1, local copies, waits for them, and re-layouts  1.32 us

profile of v5, /device:TPU:1, one launch (start us, length us, event | category | flops | bytes accessed | tf_op | source)
XLA Modules:
  0.0 36.7 jit_solution(17399801650291730797)
XLA Ops:
  0.0 35.4 %shard_map.91 = f32[64,32,256]{2,1,0:T(8,128)S(1)} custom-call(f32[64,32,256]{2,1,0:T(8,128)} %ens_ref.1, f32[32,1024]{1,0:T(8,128)} %weight_in.1, f32[1,1024]{1,0:T(1,128)} %bitcast.4, f32[1,1024]{1,0:T(1,128)} %bitcast.5, s32[1,1024]{1,0:T(1,128)} %bitcast.6, s32[4,512]{1,0:T(4,128)} %rows_in.1, s32[1,4]{1,0:T(1,128)} %bitcast.7, s32[4,256]{1,0:T(4,128)} %near_in.1, ...), custom_call_target="tpu_custom_call" | custom-call | flops 2147483648 | bytes 4194304 | tf_op jit(solution)/shard_map/pallas_call | solution.py:403
  35.4 1.3 %copy.11 = f32[64,32,256]{2,1,0:T(8,128)} copy(f32[64,32,256]{2,1,0:T(8,128)S(1)} %shard_map.91) | data formatting | bytes 4194304
